TPU v7x, 256 devices: a whole 4x4x8 slice. The times are simulated.
256 devices in a mesh: inter: 8 (over x_hi, y), intra: 8 (over z), head: 4 (over x_lo, core).
Axes of the slice: x: 4 (x_hi: 2, x_lo: 2; x = x_hi * 2 + x_lo), y: 4, z: 8, core: 2. Of those that a mesh axis runs over, the one named last changes fastest.
Arguments:
- queries: bfloat16 [32, 8192, 128], P('head', ('inter', 'intra')), parts along dimension 0, may hold values from -6 to 6
- outputs: bfloat16 [32, 8192, 128], P('head', ('inter', 'intra')), parts along dimension 0, may hold values from -6 to 6
- out_grad: bfloat16 [32, 8192, 128], P('head', ('inter', 'intra')), parts along dimension 0, may hold values from -6 to 6
- log_norm: float32 [32, 8192], P('head', ('inter', 'intra')), parts along dimension 0, may hold values from 4 to 9
- key_values: bfloat16 [8192, 512], P(('inter', 'intra'), 'head'), parts along dimension 1, may hold values from -6 to 6
- key_exponent: int32 [1024], P(('head', 'inter', 'intra')), parts along dimension 0, may hold values from -1 to 0
- value_values: bfloat16 [8192, 512], P(('inter', 'intra'), 'head'), parts along dimension 1, may hold values from -6 to 6
- value_exponent: int32 [1024], P(('head', 'inter', 'intra')), parts along dimension 0, may hold values from -2 to 1
- span_order: int32 [512], P('head'), parts along dimension 0, may hold values from 0 to 127, each once
Outputs:
- query_grad: bfloat16 [32, 8192, 128], P('head', ('inter', 'intra')), parts along dimension 0
- key_grad: bfloat16 [8192, 512], P(('inter', 'intra'), 'head'), parts along dimension 1
- value_grad: bfloat16 [8192, 512], P(('inter', 'intra'), 'head'), parts along dimension 1
There are 4 independent parts, one for each index of `head`. A program takes and returns all parts, laid end to end along the dimension named above; each array names one. Nothing has to cross between parts.
Inputs may be any that keep to these rules, and one draw needn't show every extreme that they name: `span_order`: a permutation of 0 to 127.
All inputs are finite; a program needn't handle non-finite values.
Results may differ from a plain program's by a relative error of at most 0.0049.
Values may be sent and summed in bfloat16 or wider, within the bound.
A program may use at most 64 MiB of HBM per device.

v0:
```python
import math

import jax
import jax.numpy as jnp
from jax import lax
from jax.sharding import PartitionSpec as P


def in_one_piece(arrays, axis, dim, along):
    ends, at = ([], 0)
    for a in arrays[:-1]:
        at += a.shape[along]
        ends.append(at)
    both = jnp.concatenate(arrays, axis=along)
    return tuple(jnp.split(lax.all_gather(both, axis, axis=dim, tiled=True), ends, axis=along))


def split_up(shard, dim, devices):
    dims = shard.shape
    blocks = shard.reshape(*dims[:dim], devices, dims[dim] // devices, *dims[dim + 1 :])
    return jnp.moveaxis(blocks, dim, 0)


def summed_on_arrival(shard, axis, dim):
    devices = lax.axis_size(axis)
    blocks = lax.all_to_all(split_up(shard, dim, devices), axis, 0, 0, tiled=True)
    return jnp.sum(blocks, axis=0)


def dequantize(stored, exponent):
    count, width = stored.shape
    blocks = exponent.shape[0]
    factor = jnp.exp2(exponent.astype(jnp.float32))
    shaped = (
        stored.astype(jnp.float32).reshape(blocks, count // blocks, width) * factor[:, None, None]
    )
    return shaped.reshape(count, width).astype(jnp.bfloat16)


def body(
    queries,
    outputs,
    out_grad,
    log_norm,
    key_values,
    key_exponent,
    value_values,
    value_exponent,
    span_order,
):
    heads, rows, width = queries.shape
    half = rows // 2
    scale = width ** (-0.5)
    devices = lax.axis_size(("inter", "intra"))
    total = devices * rows
    keys = dequantize(key_values, key_exponent)
    values = dequantize(value_values, value_exponent)
    index = lax.axis_index(("inter", "intra"))
    local_ids = jnp.arange(rows, dtype=jnp.int32)
    mine = lax.dynamic_slice_in_dim(span_order, 2 * index, 2, 0)
    query_pos = jnp.where(local_ids < half, mine[0], mine[1]) * half + local_ids % half
    delta = jnp.sum(out_grad.astype(jnp.float32) * outputs.astype(jnp.float32), -1)
    span_ids = jnp.arange(span_order.shape[0], dtype=jnp.int32)
    init = (
        jnp.zeros((heads, rows, width), jnp.float32),
        jnp.zeros((total, 2 * width), jnp.float32),
    )
    key_piece, value_piece = in_one_piece((keys, values), ("inter", "intra"), 0, 1)
    count = key_piece.shape[0]
    step_rows = math.gcd(count, 512)

    def advance(turn, state):
        query_acc, grads = state
        offset = turn * step_rows
        kblock = lax.dynamic_slice_in_dim(key_piece, offset, step_rows, 0)
        vblock = lax.dynamic_slice_in_dim(value_piece, offset, step_rows, 0)
        key_ids = offset + jnp.arange(step_rows, dtype=jnp.int32)
        member = (key_ids // half)[:, None] == span_ids[None, :]
        key_span = jnp.sum(jnp.where(member, span_order[None, :], 0), 1)
        key_pos = key_span * half + key_ids % half
        scores = (
            jnp.einsum("htd,kd->htk", queries, kblock, preferred_element_type=jnp.float32) * scale
        )
        live = key_pos[None, None, :] <= query_pos[None, :, None]
        probs = jnp.where(live, jnp.exp(scores - log_norm[:, :, None]), 0.0)
        probs_low = probs.astype(jnp.bfloat16)
        value_block = jnp.einsum(
            "htk,htd->kd", probs_low, out_grad, preferred_element_type=jnp.float32
        )
        dprob = jnp.einsum("htd,kd->htk", out_grad, vblock, preferred_element_type=jnp.float32)
        dscore = (probs * (dprob - delta[:, :, None])).astype(jnp.bfloat16)
        query_acc = query_acc + jnp.einsum(
            "htk,kd->htd", dscore, kblock, preferred_element_type=jnp.float32
        )
        key_block = (
            jnp.einsum("htk,htd->kd", dscore, queries, preferred_element_type=jnp.float32) * scale
        )
        joined = jnp.concatenate([key_block, value_block], 1)
        grads = lax.dynamic_update_slice_in_dim(grads, joined, offset, 0)
        return (query_acc, grads)

    query_acc, grads = lax.fori_loop(0, count // step_rows, advance, init)
    outer = lax.axis_size("inter")
    inner = lax.axis_size("intra")
    shaped = grads.reshape(outer, inner, rows, 2 * width)
    first = lax.psum_scatter(shaped, "intra", scatter_dimension=1, tiled=True)
    owned = summed_on_arrival(first, "inter", 0).reshape(rows, 2 * width)
    key_grad = owned[:, :width].astype(jnp.bfloat16)
    value_grad = owned[:, width:].astype(jnp.bfloat16)
    return ((query_acc * scale).astype(jnp.bfloat16), key_grad, value_grad)


def solution(mesh):
    return jax.shard_map(
        body,
        mesh=mesh,
        in_specs=(
            P("head", ("inter", "intra"), None),
            P("head", ("inter", "intra"), None),
            P("head", ("inter", "intra"), None),
            P("head", ("inter", "intra")),
            P(("inter", "intra"), "head"),
            P(("head", "inter", "intra")),
            P(("inter", "intra"), "head"),
            P(("head", "inter", "intra")),
            P("head"),
        ),
        out_specs=(
            P("head", ("inter", "intra"), None),
            P(("inter", "intra"), "head"),
            P(("inter", "intra"), "head"),
        ),
        check_vma=False,
    )
```

profile of v0, /device:TPU:2, one launch (start us, length us, event | category | flops | bytes accessed | tf_op | source)
XLA Modules:
  0.0 413.2 jit_solution(4231447524439005689)
XLA Ops:
  15.3 127.1 %all-gather.2.cloned.1.call-done = bf16[8192,256]{1,0:T(8,128)(2,1)} async-done(((bf16[128,256]{1,0:T(8,128)(2,1)}), bf16[8192,256]{1,0:T(8,128)(2,1)}) %all-gather.2.cloned.1.call-update) | async-done | bytes 4194320 | tf_op jit(solution)/shard_map/all_gather | solution.py:15
  142.5 4.4 %fusion.22 = (bf16[8192,128]{1,0:T(8,128)(2,1)}, bf16[8192,128]{1,0:T(8,128)(2,1)}) fusion(bf16[8192,256]{1,0:T(8,128)(2,1)} %all-gather.2.cloned.1.call-done), kind=kLoop, calls=%fused_computation.46 | loop fusion | bytes 8388608 | tf_op jit(solution)/shard_map/split | solution.py:15
  146.9 3.8 broadcast_in_dim.101.clone
  150.7 129.8 %while.18 = (s32[]{:T(128)}, f32[8,128,128]{2,1,0:T(8,128)S(1)}, f32[8192,256]{1,0:T(8,128)}, s32[128]{0:T(128)S(1)}, bf16[8192,128]{1,0:T(8,128)(2,1)}, /*index...) while((s32[]{:T(128)}, f32[8,128,128]{2,1,0:T(8,128)S(1)}, ...), condition=%wide.region_3.4_spmd.clone, body=%wide.region_1.3_spmd.clone.sunk | while | flops 675495680 | bytes 15750901 | solution.py:102
  156.2 1.6 convolution_add_fusion.2
  164.3 1.6 convolution_add_fusion.2
  172.4 1.6 convolution_add_fusion.2
  180.5 1.6 convolution_add_fusion.2
  188.6 1.6 convolution_add_fusion.2
  196.7 1.6 convolution_add_fusion.2
  204.8 1.6 convolution_add_fusion.2
  212.9 1.6 convolution_add_fusion.2
  221.0 1.6 convolution_add_fusion.2
  229.1 1.6 convolution_add_fusion.2
  237.3 1.6 convolution_add_fusion.2
  245.4 1.6 convolution_add_fusion.2
  253.5 1.6 convolution_add_fusion.2
  261.6 1.6 convolution_add_fusion.2
  269.7 1.6 convolution_add_fusion.2
  280.5 7.6 %copy.51 = f32[8,8,128,256]{3,2,0,1:T(8,128)} copy(f32[8,8,128,256]{3,2,1,0:T(8,128)} %bitcast.56) | data formatting | bytes 16777216 | tf_op jit(solution)/shard_map/reshape | solution.py:105
  288.2 92.4 %reduce-scatter.2.cloned.1.call-done = f32[8,1,128,256]{3,2,0,1:T(8,128)} async-done(((f32[8,8,128,256]{3,2,0,1:T(8,128)}), f32[8,1,128,256]{3,2,0,1:T(8,128)}) %reduce-scatter.2.cloned.1.call-update) | async-done | bytes 1048592 | tf_op jit(solution)/shard_map/reduce_scatter | solution.py:106
  380.5 2.6 copy.52
  383.1 5.8 %all-to-all-start = ((f32[8,1,1,128,256]{3,4,2,1,0:T(8,128)}), f32[8,1,1,128,256]{3,4,2,1,0:T(8,128)S(1)}, u32[]{:S(2)}, u32[]{:S(2)}) async-start(f32[8,1,1,128,256]{3,4,2,1,0:T(8,128)} %copy.52), calls=%async_computation.1 | async-start | bytes 2097152 | tf_op jit(solution)/shard_map/all_to_all | solution.py:26
  389.7 15.1 %all-to-all-done = f32[8,1,1,128,256]{3,4,2,1,0:T(8,128)S(1)} async-done(((f32[8,1,1,128,256]{3,4,2,1,0:T(8,128)}), f32[8,1,1,128,256]{3,4,2,1,0:T(8,128)S(1)}, u32[]{:S(2)}, u32[]{:S(2)}) %all-to-all-start) | async-done | bytes 1048608 | tf_op jit(solution)/shard_map/all_to_all | solution.py:26
  (220 shorter events, 115.7 us)
Async XLA Ops:
  7.2 135.3 %all-gather.2.cloned.1.call-start = ((), (), s32[]{:S(2)}) async-start(), calls=%async_computation.2 | async-start | bytes 4259840 | tf_op jit(solution)/shard_map/all_gather | solution.py:15
  10.4 370.1 %reduce-scatter.2.cloned.1.call-start = ((), (), s32[]{:S(2)}) async-start(), calls=%async_computation.3 | async-start | bytes 9437184 | tf_op jit(solution)/shard_map/reduce_scatter | solution.py:106
  146.9 3.8 copy-start
  146.9 3.8 copy-start.1
  383.1 21.7 %all-to-all-start = ((f32[8,1,1,128,256]{3,4,2,1,0:T(8,128)}), f32[8,1,1,128,256]{3,4,2,1,0:T(8,128)S(1)}, u32[]{:S(2)}, u32[]{:S(2)}) async-start(f32[8,1,1,128,256]{3,4,2,1,0:T(8,128)} %copy.52), calls=%async_computation.1 | async-start | bytes 2097152 | tf_op jit(solution)/shard_map/all_to_all | solution.py:26
Sparse Core Ops, SparseCore 0:
  12.1 130.3 all-gather.1
  288.3 92.1 reduce-scatter.1
where the time goes:
time: 415 us; the launch traced here: 413 us
  waiting for transfers between devices  235 us (57%)
  matrix products  84.7 us (20%)
  local copies, waits for them, and re-layouts  40.3 us (10%)
  other arithmetic  32.3 us (8%)
  between operations  14.1 us (3%)
  starting transfers between devices  5.9 us (1%)
    all_gather x1, waiting for transfers between devices, in_one_piece(): lax.all_gather(both, axis, axis=dim, tiled=True)  127 us
    reduce_scatter x1, waiting for transfers between devices, body(): first = lax.psum_scatter(shaped, 'intra', scatter_dimension=1, tiled=True)  92.4 us
    dot_general x16, matrix products, advance(): jnp.einsum('htk,kd->htd', dscore, kblock, preferred_element_type=jnp.floa...  24.9 us
    dot_general x16, matrix products, advance(): jnp.einsum('htd,kd->htk', queries, kblock, preferred_element_type=jnp.flo...  23.3 us
    dot_general x16, matrix products, advance(): jnp.einsum('htd,kd->htk', out_grad, vblock, preferred_element_type=jnp.fl...  21.3 us
    add x16, other arithmetic, body(): jnp.where(local_ids < half, mine[0], mine[1]) * half + local_ids % half  20.5 us
    dynamic_update_slice x32, local copies, waits for them, and re-layouts, advance(): grads = lax.dynamic_update_slice_in_dim(grads, joined, offset, 0)  16.6 us
    all_to_all x1, waiting for transfers between devices, summed_on_arrival(): lax.all_to_all(split_up(shard, dim, devices), axis, 0, 0, tiled=True)  15.1 us
  transfers between devices with their start and end apart: 3, of which 3 were waited for; matrix products, arithmetic and copies ran while one was open for 1% of the time, Pallas kernels for 0%

commit v1 on v0

v1 whole, which is shorter than its diff:
```python
import math

import jax
import jax.numpy as jnp
from jax import lax
from jax.experimental import pallas as pl
from jax.experimental.pallas import tpu as pltpu
from jax.sharding import PartitionSpec as P

MESH = pl.DeviceIdType.MESH
F32, BF16 = jnp.float32, jnp.bfloat16
NT = (((1,), (1,)), ((), ()))
NN = (((1,), (0,)), ((), ()))
TN = (((0,), (0,)), ((), ()))
ROWS = 128
HALF = 64
WIDTH = 128
UNIT = 512
NX, NY, NZ = 2, 4, 8
MASKED = -(2.0**100)

ORDER = (
    (0, 0), (0, 1), (7, 0), (1, 0),
    (7, 1), (1, 1), (6, 0), (2, 0),
    (6, 1), (2, 1), (5, 0), (3, 0),
    (5, 1), (3, 1), (4, 0), (4, 1),
)
GROUP = 4
PAIRS = (0, 1, 1, 0, 1, 2, 0, 1, 2, 2, 3, 3, 2, 3, 3)
GROUPS = (1, 0, 1, 2, 2, 0, 3, 3, 3, 2, 3, 2, 1, 1, 0)


def slot(rel, column):
    return ORDER.index((rel % NZ, column))


def packed(digits):
    return sum(d * 4**n for n, d in enumerate(digits))


def dot(a, b, dims):
    return lax.dot_general(a, b, dims, preferred_element_type=F32)


def in_three(x):
    high = x.astype(BF16).astype(F32)
    rest = x - high
    mid = rest.astype(BF16).astype(F32)
    return high, mid, (rest - mid).astype(BF16).astype(F32)


def kernel(
    q_in,
    do_in,
    o_in,
    lse_in,
    k_in,
    v_in,
    kexp,
    vexp,
    spans,
    dq_out,
    dk_out,
    dv_out,
    qb,
    dob,
    ext,
    aux,
    kv,
    kext,
    vext,
    dq,
    dkv,
    kvs,
    kvr,
    last,
    xr,
    dqs,
    dqr,
    load_sem,
    kv_send,
    kv_recv,
    q_send,
    q_recv,
    aux_send,
    aux_recv,
    red_send,
    red_recv,
    last_recv,
    x_send,
    x_recv,
    dq_send,
    dq_recv,
):
    scale = WIDTH**-0.5
    root = WIDTH**0.5
    factor = scale * math.log2(math.e)
    inter, z, head = lax.axis_index("inter"), lax.axis_index("intra"), lax.axis_index("head")
    x, y = inter // NY, inter % NY

    def at(dx, dy, dz):
        return ((x + dx) % NX) * NY + (y + dy) % NY, (z + dz) % NZ

    def device(dx, dy, dz):
        return (*at(dx, dy, dz), head)

    UP, DOWN, ACROSS = device(0, 1, 0), device(0, -1, 0), device(0, 2, 0)
    RIGHT, LEFT, OTHER = device(0, 0, 1), device(0, 0, -1), device(1, 0, 0)

    def rows(index, size):
        return pl.ds(index * size, size)

    loads = []
    for u in range(2):
        for n, (src, dst) in enumerate(((q_in, qb), (do_in, dob))):
            loads.append(
                pltpu.make_async_copy(src.at[rows(u, UNIT)], dst.at[rows(u, UNIT)], load_sem.at[u, n])
            )
            loads[-1].start()

    barrier = pltpu.get_barrier_semaphore()
    for peer in (UP, DOWN, ACROSS, RIGHT, LEFT, OTHER):
        pl.semaphore_signal(barrier, inc=1, device_id=peer, device_id_type=MESH)

    def power(e):
        return jnp.where(e == -2, 0.25, jnp.where(e == -1, 0.5, jnp.where(e == 0, 1.0, 2.0)))

    block = ROWS // 4
    for b in range(4):
        r = rows(b, block)
        kv[r, :WIDTH] = (k_in[r, :].astype(F32) * power(kexp[b])).astype(BF16)
        kv[r, WIDTH:] = (v_in[r, :].astype(F32) * power(vexp[b])).astype(BF16)

    pl.semaphore_wait(barrier, 6)

    pending = []

    def send(src, dst, ssem, rsem, peer):
        def copy():
            return pltpu.make_async_remote_copy(
                src_ref=src(), dst_ref=dst(), send_sem=ssem(), recv_sem=rsem(), device_id=peer, device_id_type=MESH
            )

        copy().start()
        pending.append(copy)

    def arrived(dst, rsem):
        pltpu.make_async_remote_copy(
            src_ref=dst, dst_ref=dst, send_sem=rsem, recv_sem=rsem, device_id=UP, device_id_type=MESH
        ).wait_recv()

    def kv_go(way, src, dst):
        peer = (RIGHT, LEFT, OTHER)[way]
        send(
            lambda: kv.at[rows(src, ROWS)],
            lambda: kv.at[rows(dst, ROWS)],
            lambda: kv_send.at[way, src],
            lambda: kv_recv.at[dst],
            peer,
        )

    def kv_here(rel, column):
        s = slot(rel, column)
        arrived(kv.at[rows(s, ROWS)], kv_recv.at[s])

    def kv_pass(rel, column):
        kv_here(rel, column)
        s = slot(rel, column)
        if rel > 4:
            kv_go(0, s, slot(rel - 1, column))
        else:
            kv_go(1, s, slot(rel + 1, column))

    def q_go(src, dst, index, peer):
        for n, buf in enumerate((qb, dob)):
            send(
                lambda buf=buf: buf.at[rows(src, UNIT)],
                lambda buf=buf: buf.at[rows(dst, UNIT)],
                lambda n=n: q_send.at[index, n],
                lambda n=n: q_recv.at[dst, n],
                peer,
            )

    def q_here(u):
        for n, buf in enumerate((qb, dob)):
            arrived(buf.at[rows(u, UNIT)], q_recv.at[u, n])

    kv_go(2, 0, 1)
    kv_go(0, 0, slot(7, 0))
    kv_go(1, 0, slot(1, 0))
    for copy in loads:
        copy.wait()
    q_go(0, 2, 0, DOWN)
    q_go(1, 3, 1, UP)

    aux[0, 0] = lse_in[...] * root
    ones = jnp.ones((8, WIDTH), BF16)
    for u in range(2):
        r = rows(u, UNIT)
        prod = dob[r, :].astype(F32) * o_in[r, :].astype(F32)
        high = prod.astype(BF16)
        low = (prod - high.astype(F32)).astype(BF16)
        total = dot(ones, high, NT) + dot(ones, low, NT)
        for h in range(4):
            aux[0, 1, 4 * u + h : 4 * u + h + 1, :] = total[0:1, h * ROWS : (h + 1) * ROWS]
    for n, (dst, peer) in enumerate(((2, UP), (1, DOWN), (3, ACROSS))):
        send(
            lambda: aux.at[0],
            lambda dst=dst: aux.at[dst],
            lambda n=n: aux_send.at[n],
            lambda dst=dst: aux_recv.at[dst],
            peer,
        )

    q_go(1, 4, 2, DOWN)
    q_go(0, 5, 3, UP)

    def build_ext(u, b, first_head):
        row = lax.broadcasted_iota(jnp.int32, (16, ROWS), 0)
        lane = lax.broadcasted_iota(jnp.int32, (16, ROWS), 1)
        member = jnp.where(row == 6 + 2 * b + lane // HALF, 1.0, 0.0)
        for h in range(4):
            hh = first_head + h
            parts = in_three(aux[b, 0, hh : hh + 1, :]) + in_three(aux[b, 1, hh : hh + 1, :])
            m = member
            for n, part in enumerate(parts):
                m = jnp.where(row == n, part, m)
            m = jnp.concatenate([m, jnp.zeros((ROWS - 16, ROWS), F32)], 0)
            ext[pl.ds(u * UNIT + h * ROWS, ROWS), :] = m.T.astype(BF16)

    lanes = lax.broadcasted_iota(jnp.int32, (ROWS, WIDTH), 1)
    upper = lax.broadcasted_iota(jnp.int32, (ROWS, WIDTH), 0) >= HALF
    q_span = jnp.full((ROWS, WIDTH), 2**20, jnp.int32)
    for b, dy in enumerate((0, 1, -1, 2)):
        i, k = at(0, dy, 0)
        for n in range(2):
            q_span = jnp.where(lanes == 6 + 2 * b + n, spans[2 * (i * NZ + k) + n], q_span)
    base = jnp.where(lanes < 3, -1.0, 0.0)

    def build_kext(s):
        rel, column = ORDER[s]
        i, k = at(column, 0, rel)
        first = 2 * (i * NZ + k)
        k_span = jnp.where(upper, spans[first + 1], spans[first])
        kext[rows(s, ROWS), :] = jnp.where(k_span > q_span, MASKED, base).astype(BF16)

    def tile(units, s0, ns, diagonal=False):
        nk = ns * ROWS
        r = pl.ds(s0 * ROWS, nk)
        k = kv[r, :WIDTH]
        ka = jnp.concatenate([k, kext[r, :]], 1)
        va = jnp.concatenate([kv[r, WIDTH:], vext[:nk, :]], 1)
        ru = pl.ds(units * 2 * UNIT, 2 * UNIT)
        q, do, e = qb[ru, :], dob[ru, :], ext[ru, :]
        scores = dot(ka, jnp.concatenate([q, e], 1), NT)
        diff = dot(va, jnp.concatenate([do, e], 1), NT)
        probs = jnp.exp2(scores * factor)
        if diagonal:
            a = lax.broadcasted_iota(jnp.int32, (nk, 2 * UNIT), 0)
            t = lax.broadcasted_iota(jnp.int32, (nk, 2 * UNIT), 1) % ROWS
            probs = jnp.where((a // HALF != t // HALF) | (a <= t), probs, 0.0)
        low = probs.astype(BF16)
        ds = (probs * diff).astype(BF16)
        dkv[r, WIDTH:] += dot(low, do, NN)
        dkv[r, :WIDTH] += dot(ds, q, NN)
        dq[ru, :] += dot(ds, k, TN)

    def reduce_go(rel, column):
        s = slot(rel, column)
        r = rows(s, ROWS)
        total = dkv[r, :]
        if not (rel == 4 or (rel, column) in ((5, 1), (3, 0))):
            arrived(kvr.at[r], red_recv.at[s])
            total = total + kvr[r, :].astype(F32)
        left = rel > 4 or (rel == 4 and column == 0)
        peer = LEFT if left else RIGHT
        if rel in (1, 7):
            dkv[r, :] = total
            n = 2 * column + (rel == 1)
            send(
                lambda: dkv.at[rows(s, ROWS)],
                lambda: last.at[rows(n, ROWS)],
                lambda: red_send.at[s],
                lambda: last_recv.at[n],
                peer,
            )
        else:
            kvs[r, :] = total.astype(BF16)
            dst = slot(rel + 1 if left else rel - 1, column)
            send(
                lambda: kvs.at[rows(s, ROWS)],
                lambda: kvr.at[rows(dst, ROWS)],
                lambda: red_send.at[s],
                lambda: red_recv.at[dst],
                peer,
            )

    def dq_go(u, peer):
        r = rows(u - 2, UNIT)
        dqs[r, :] = dq[rows(u, UNIT), :].astype(BF16)
        send(
            lambda: dqs.at[rows(u - 2, UNIT)],
            lambda: dqr.at[rows(u - 2, UNIT)],
            lambda: dq_send.at[u - 2],
            lambda: dq_recv.at[u - 2],
            peer,
        )

    def own_total(column):
        total = dkv[rows(column, ROWS), :]
        for n in (2 * column, 2 * column + 1):
            arrived(last.at[rows(n, ROWS)], last_recv.at[n])
            total = total + last[rows(n, ROWS), :]
        return total

    kv_here(0, 1)
    kv_go(0, 1, slot(7, 1))
    kv_go(1, 1, slot(1, 1))
    kv_pass(7, 0)
    kv_pass(1, 0)
    for s in range(16):
        build_kext(s)
    build_ext(0, 0, 0)
    build_ext(1, 0, 4)
    wide = lax.broadcasted_iota(jnp.int32, vext.shape, 1)
    vext[...] = jnp.where((wide >= 3) & (wide < 6), -1.0, 0.0).astype(BF16)
    dq[...] = jnp.zeros_like(dq)
    dkv[...] = jnp.zeros_like(dkv)
    tile(0, 0, 1, diagonal=True)
    tile(0, 1, 3)

    def before_0():
        for rel, column in ORDER[4:8]:
            kv_pass(rel, column)

    def before_1():
        for n in (1, 2):
            arrived(aux.at[n], aux_recv.at[n])
        q_go(0, 6, 4, ACROSS)
        q_go(1, 7, 5, ACROSS)
        q_here(2)
        q_here(3)
        build_ext(2, 1, 0)
        build_ext(3, 2, 4)

    def before_2():
        kv_pass(6, 1)
        kv_pass(2, 1)
        kv_pass(5, 0)
        kv_here(3, 0)

    def before_4():
        kv_pass(3, 1)

    def before_5():
        q_here(4)
        q_here(5)
        build_ext(4, 1, 4)
        build_ext(5, 2, 0)

    def before_6():
        kv_here(5, 1)
        kv_here(4, 0)
        kv_here(4, 1)

    def before_8():
        dq_go(2, UP)
        dq_go(3, DOWN)

    def before_10():
        arrived(aux.at[3], aux_recv.at[3])
        q_here(6)
        q_here(7)
        build_ext(6, 3, 0)
        build_ext(7, 3, 4)

    def before_11():
        for rel, column in ((4, 0), (4, 1), (5, 1)):
            reduce_go(rel, column)

    def before_12():
        for rel, column in ((3, 1), (3, 0), (5, 0), (6, 1), (2, 1)):
            reduce_go(rel, column)

    def before_13():
        dq_go(4, UP)
        dq_go(5, DOWN)

    def before_14():
        for rel, column in ((7, 1), (1, 1), (6, 0), (2, 0)):
            reduce_go(rel, column)

    between = {
        0: before_0,
        1: before_1,
        2: before_2,
        4: before_4,
        5: before_5,
        6: before_6,
        8: before_8,
        10: before_10,
        11: before_11,
        12: before_12,
        13: before_13,
        14: before_14,
    }

    def step(i, codes):
        pair, group = codes
        for n, act in between.items():
            pl.when(i == n)(act)
        tile(pair % 4, (group % 4) * GROUP, GROUP)
        return pair // 4, group // 4

    lax.fori_loop(0, len(PAIRS), step, (jnp.int32(packed(PAIRS)), jnp.int32(packed(GROUPS))))

    dq_go(6, ACROSS)
    dq_go(7, ACROSS)
    reduce_go(7, 0)
    reduce_go(1, 0)
    r = rows(1, ROWS)
    dkv[r, :] = own_total(1)
    send(lambda: dkv.at[rows(1, ROWS)], lambda: xr, lambda: x_send, lambda: x_recv, OTHER)
    mine = own_total(0)
    arrived(xr, x_recv)
    mine = mine + xr[...]
    dk_out[...] = (mine[:, :WIDTH] * scale).astype(BF16)
    dv_out[...] = mine[:, WIDTH:].astype(BF16)
    for u, terms in ((0, (2, 5, 6)), (1, (3, 4, 7))):
        total = dq[rows(u, UNIT), :]
        for n in terms:
            r = rows(n - 2, UNIT)
            arrived(dqr.at[r], dq_recv.at[n - 2])
            total = total + dqr[r, :].astype(F32)
        dq_out[rows(u, UNIT), :] = (total * scale).astype(BF16)
    for copy in pending:
        copy().wait_send()


def body(
    queries,
    outputs,
    out_grad,
    log_norm,
    key_values,
    key_exponent,
    value_values,
    value_exponent,
    span_order,
):
    heads, tokens, width = queries.shape
    flat = (heads * tokens, width)
    vmem = pl.BlockSpec(memory_space=pltpu.VMEM)
    smem = pl.BlockSpec(memory_space=pltpu.SMEM)
    hbm = pl.BlockSpec(memory_space=pl.ANY)
    dma = pltpu.SemaphoreType.DMA
    units = 8 * UNIT
    keys = 16 * ROWS
    query_grad, key_grad, value_grad = pl.pallas_call(
        kernel,
        out_shape=(
            jax.ShapeDtypeStruct(flat, BF16),
            jax.ShapeDtypeStruct((tokens, width), BF16),
            jax.ShapeDtypeStruct((tokens, width), BF16),
        ),
        in_specs=[hbm, hbm, vmem, vmem, vmem, vmem, smem, smem, smem],
        out_specs=(vmem, vmem, vmem),
        scratch_shapes=[
            pltpu.VMEM((units, width), BF16),
            pltpu.VMEM((units, width), BF16),
            pltpu.VMEM((units, width), BF16),
            pltpu.VMEM((4, 2, heads, tokens), F32),
            pltpu.VMEM((keys, 2 * width), BF16),
            pltpu.VMEM((keys, width), BF16),
            pltpu.VMEM((GROUP * ROWS, width), BF16),
            pltpu.VMEM((units, width), F32),
            pltpu.VMEM((keys, 2 * width), F32),
            pltpu.VMEM((keys, 2 * width), BF16),
            pltpu.VMEM((keys, 2 * width), BF16),
            pltpu.VMEM((4 * ROWS, 2 * width), F32),
            pltpu.VMEM((ROWS, 2 * width), F32),
            pltpu.VMEM((6 * UNIT, width), BF16),
            pltpu.VMEM((6 * UNIT, width), BF16),
            dma((2, 2)),
            dma((3, 16)),
            dma((16,)),
            dma((6, 2)),
            dma((8, 2)),
            dma((3,)),
            dma((4,)),
            dma((16,)),
            dma((16,)),
            dma((4,)),
            dma,
            dma,
            dma((6,)),
            dma((6,)),
        ],
        compiler_params=pltpu.CompilerParams(
            collective_id=0, has_side_effects=True, vmem_limit_bytes=56 * 2**20
        ),
        cost_estimate=pl.CostEstimate(
            flops=10 * heads * tokens * 64 * tokens * width,
            bytes_accessed=8 * heads * tokens * width,
            transcendentals=heads * tokens * 64 * tokens,
        ),
        name="attention_backward",
    )(
        queries.reshape(flat),
        out_grad.reshape(flat),
        outputs.reshape(flat),
        log_norm,
        key_values,
        value_values,
        key_exponent,
        value_exponent,
        span_order,
    )
    return query_grad.reshape(heads, tokens, width), key_grad, value_grad


def solution(mesh):
    return jax.shard_map(
        body,
        mesh=mesh,
        in_specs=(
            P("head", ("inter", "intra"), None),
            P("head", ("inter", "intra"), None),
            P("head", ("inter", "intra"), None),
            P("head", ("inter", "intra")),
            P(("inter", "intra"), "head"),
            P(("head", "inter", "intra")),
            P(("inter", "intra"), "head"),
            P(("head", "inter", "intra")),
            P("head"),
        ),
        out_specs=(
            P("head", ("inter", "intra"), None),
            P(("inter", "intra"), "head"),
            P(("inter", "intra"), "head"),
        ),
        check_vma=False,
    )
```

time: 415 us -> 66.7 us (0.16)
  waiting for transfers between devices: 235 us -> 0 us
  matrix products: 84.7 us -> 0 us
  Pallas kernels: 0 us -> 62.3 us
  local copies, waits for them, and re-layouts: 40.3 us -> 3.06 us
  other arithmetic: 32.3 us -> 0 us
  between operations: 14.1 us -> 0.65 us
  starting transfers between devices: 5.9 us -> 0 us
    all_gather x1 -> x0, waiting for transfers between devices: 127 us -> none  [in_one_piece(): lax.all_gather(both, axis, axis=dim, tiled=True)]
    reduce_scatter x1 -> x0, waiting for transfers between devices: 92.4 us -> none  [body(): first = lax.psum_scatter(shaped, 'intra', scatter_dimension=1, tiled=True)]
    dot_general x80 -> x0, matrix products: 84.7 us -> none  [the longest x16 24.9 us: advance(): jnp.einsum('htk,kd->htd', dscore, kblock, preferred_element_type=jnp.floa...]
    pallas_call x0 -> x1, Pallas kernels: none -> 62.3 us  [body(): pl.pallas_call(kernel, out_shape=(jax.ShapeDtypeStruct(flat, BF16), jax.S...]
    add x32 -> x0, other arithmetic: 20.7 us -> none  [the longest x16 20.5 us: body(): jnp.where(local_ids < half, mine[0], mine[1]) * half + local_ids % half]
    dynamic_update_slice x32 -> x0, local copies, waits for them, and re-layouts: 16.6 us -> none  [advance(): grads = lax.dynamic_update_slice_in_dim(grads, joined, offset, 0)]
    all_to_all x1 -> x0, waiting for transfers between devices: 15.1 us -> none  [summed_on_arrival(): lax.all_to_all(split_up(shard, dim, devices), axis, 0, 0, tiled=True)]
    reshape x2 -> x0, local copies, waits for them, and re-layouts: 10.2 us -> none  [the longest x1 7.6 us: body(): shaped = grads.reshape(outer, inner, rows, 2 * width)]
  transfers between devices with their start and end apart: 3 -> 0, of which waited for: 3 -> 0; matrix products, arithmetic and copies ran while one was open for 1% -> 0% of each run, Pallas kernels for 0% -> 0%
where the time goes in v1:
time: 66.7 us; the launch traced here: 66 us
  Pallas kernels  62.3 us (93%)
  local copies, waits for them, and re-layouts  3.06 us (5%)
    pallas_call x1, Pallas kernels, body(): pl.pallas_call(kernel, out_shape=(jax.ShapeDtypeStruct(flat, BF16), jax.S...  62.3 us
    unnamed x7, local copies, waits for them, and re-layouts  3.06 us

profile of v1, /device:TPU:2, one launch (start us, length us, event | category | flops | bytes accessed | tf_op | source)
XLA Modules:
  0.0 66.0 jit_solution(7251694815669983095)
XLA Ops:
  0.6 62.3 %attention_backward.1 = (bf16[1024,128]{1,0:T(8,128)(2,1)}, bf16[128,128]{1,0:T(8,128)(2,1)}, bf16[128,128]{1,0:T(8,128)(2,1)}) custom-call(bf16[1024,128]{1,0:T(8,128)(2,1)} %bitcast.5, bf16[1024,128]{1,0:T(8,128)(2,1)} %bitcast.6, bf16[1024,128]{1,0:T(8,128)(2,1)} %bitcast.7, f32[8,128]{1,0:T(8,128)} %lse_in.1, bf16[128,128]{1,0:T(8,128)(2,1)} %k_in.1, ...), custom_call_target="tpu_custom_call" | custom-call | flops 10737418240 | bytes 1048576 | tf_op jit(solution)/shard_map/attention_backward/pallas_call | solution.py:459
  62.9 0.0 copy-start.1
  63.0 1.7 %copy.15 = bf16[8,128,128]{2,1,0:T(8,128)(2,1)} copy(bf16[8,128,128]{2,1,0:T(8,128)(2,1)} %bitcast.4) | data formatting | bytes 524288
  64.6 0.0 copy-done.1
  64.6 0.0 copy-start
  64.6 0.6 copy.16
  65.3 0.2 copy-done
  65.4 0.6 copy.17
Async XLA Ops:
  62.9 1.7 %copy-start.1 = (bf16[128,128]{1,0:T(8,128)(2,1)S(1)}, bf16[128,128]{1,0:T(8,128)(2,1)}, u32[]{:S(2)}) copy-start(bf16[128,128]{1,0:T(8,128)(2,1)} %get-tuple-element.13) | copy-start | bytes 98308
  64.6 0.8 %copy-start = (bf16[128,128]{1,0:T(8,128)(2,1)S(1)}, bf16[128,128]{1,0:T(8,128)(2,1)}, u32[]{:S(2)}) copy-start(bf16[128,128]{1,0:T(8,128)(2,1)} %get-tuple-element.14) | copy-start | bytes 98308

commit v2 on v1

--- a/solution.py
+++ b/solution.py
@@ -26,8 +26,8 @@
     (5, 1), (3, 1), (4, 0), (4, 1),
 )
 GROUP = 4
-PAIRS = (0, 1, 1, 0, 1, 2, 0, 1, 2, 2, 3, 3, 2, 3, 3)
-GROUPS = (1, 0, 1, 2, 2, 0, 3, 3, 3, 2, 3, 2, 1, 1, 0)
+PAIRS = (0, 1, 1, 0, 1, 2, 2, 0, 1, 2, 3, 3, 2, 3, 3)
+GROUPS = (1, 0, 1, 2, 2, 0, 2, 3, 3, 3, 3, 2, 1, 1, 0)
 
 
 def slot(rel, column):
@@ -106,6 +106,7 @@
 
     UP, DOWN, ACROSS = device(0, 1, 0), device(0, -1, 0), device(0, 2, 0)
     RIGHT, LEFT, OTHER = device(0, 0, 1), device(0, 0, -1), device(1, 0, 0)
+    RIGHT2, LEFT2 = device(0, 0, 2), device(0, 0, -2)
 
     def rows(index, size):
         return pl.ds(index * size, size)
@@ -119,7 +120,7 @@
             loads[-1].start()
 
     barrier = pltpu.get_barrier_semaphore()
-    for peer in (UP, DOWN, ACROSS, RIGHT, LEFT, OTHER):
+    for peer in (UP, DOWN, ACROSS, RIGHT, LEFT, RIGHT2, LEFT2, OTHER):
         pl.semaphore_signal(barrier, inc=1, device_id=peer, device_id_type=MESH)
 
     def power(e):
@@ -131,7 +132,7 @@
         kv[r, :WIDTH] = (k_in[r, :].astype(F32) * power(kexp[b])).astype(BF16)
         kv[r, WIDTH:] = (v_in[r, :].astype(F32) * power(vexp[b])).astype(BF16)
 
-    pl.semaphore_wait(barrier, 6)
+    pl.semaphore_wait(barrier, 8)
 
     pending = []
 
@@ -150,7 +151,7 @@
         ).wait_recv()
 
     def kv_go(way, src, dst):
-        peer = (RIGHT, LEFT, OTHER)[way]
+        peer = (RIGHT, LEFT, OTHER, RIGHT2, LEFT2)[way]
         send(
             lambda: kv.at[rows(src, ROWS)],
             lambda: kv.at[rows(dst, ROWS)],
@@ -163,13 +164,22 @@
         s = slot(rel, column)
         arrived(kv.at[rows(s, ROWS)], kv_recv.at[s])
 
-    def kv_pass(rel, column):
+    def kv_near(column):
+        s = slot(0, column)
+        for way, rel in ((0, 7), (1, 1), (3, 6), (4, 2)):
+            kv_go(way, s, slot(rel, column))
+
+    def kv_far(rel, column):
         kv_here(rel, column)
         s = slot(rel, column)
-        if rel > 4:
-            kv_go(0, s, slot(rel - 1, column))
+        if rel == 6:
+            kv_go(0, s, slot(5, column))
+            if column == 0:
+                kv_go(3, s, slot(4, column))
         else:
-            kv_go(1, s, slot(rel + 1, column))
+            kv_go(1, s, slot(3, column))
+            if column == 1:
+                kv_go(4, s, slot(4, column))
 
     def q_go(src, dst, index, peer):
         for n, buf in enumerate((qb, dob)):
@@ -186,8 +196,7 @@
             arrived(buf.at[rows(u, UNIT)], q_recv.at[u, n])
 
     kv_go(2, 0, 1)
-    kv_go(0, 0, slot(7, 0))
-    kv_go(1, 0, slot(1, 0))
+    kv_near(0)
     for copy in loads:
         copy.wait()
     q_go(0, 2, 0, DOWN)
@@ -212,9 +221,6 @@
             peer,
         )
 
-    q_go(1, 4, 2, DOWN)
-    q_go(0, 5, 3, UP)
-
     def build_ext(u, b, first_head):
         row = lax.broadcasted_iota(jnp.int32, (16, ROWS), 0)
         lane = lax.broadcasted_iota(jnp.int32, (16, ROWS), 1)
@@ -227,22 +233,6 @@
                 m = jnp.where(row == n, part, m)
             m = jnp.concatenate([m, jnp.zeros((ROWS - 16, ROWS), F32)], 0)
             ext[pl.ds(u * UNIT + h * ROWS, ROWS), :] = m.T.astype(BF16)
-
-    lanes = lax.broadcasted_iota(jnp.int32, (ROWS, WIDTH), 1)
-    upper = lax.broadcasted_iota(jnp.int32, (ROWS, WIDTH), 0) >= HALF
-    q_span = jnp.full((ROWS, WIDTH), 2**20, jnp.int32)
-    for b, dy in enumerate((0, 1, -1, 2)):
-        i, k = at(0, dy, 0)
-        for n in range(2):
-            q_span = jnp.where(lanes == 6 + 2 * b + n, spans[2 * (i * NZ + k) + n], q_span)
-    base = jnp.where(lanes < 3, -1.0, 0.0)
-
-    def build_kext(s):
-        rel, column = ORDER[s]
-        i, k = at(column, 0, rel)
-        first = 2 * (i * NZ + k)
-        k_span = jnp.where(upper, spans[first + 1], spans[first])
-        kext[rows(s, ROWS), :] = jnp.where(k_span > q_span, MASKED, base).astype(BF16)
 
     def tile(units, s0, ns, diagonal=False):
         nk = ns * ROWS
@@ -313,44 +303,63 @@
             total = total + last[rows(n, ROWS), :]
         return total
 
-    kv_here(0, 1)
-    kv_go(0, 1, slot(7, 1))
-    kv_go(1, 1, slot(1, 1))
-    kv_pass(7, 0)
-    kv_pass(1, 0)
+    lanes = lax.broadcasted_iota(jnp.int32, (ROWS, WIDTH), 1)
+    upper = lax.broadcasted_iota(jnp.int32, (ROWS, WIDTH), 0) >= HALF
+    q_span = jnp.full((ROWS, WIDTH), 2**20, jnp.int32)
+    for b, dy in enumerate((0, 1, -1, 2)):
+        i, k = at(0, dy, 0)
+        for n in range(2):
+            q_span = jnp.where(lanes == 6 + 2 * b + n, spans[2 * (i * NZ + k) + n], q_span)
+    base = jnp.where(lanes < 3, -1.0, 0.0)
+
+    def build_kext(s):
+        rel, column = ORDER[s]
+        i, k = at(column, 0, rel)
+        first = 2 * (i * NZ + k)
+        k_span = jnp.where(upper, spans[first + 1], spans[first])
+        kext[rows(s, ROWS), :] = jnp.where(k_span > q_span, MASKED, base).astype(BF16)
+
     for s in range(16):
         build_kext(s)
-    build_ext(0, 0, 0)
-    build_ext(1, 0, 4)
     wide = lax.broadcasted_iota(jnp.int32, vext.shape, 1)
     vext[...] = jnp.where((wide >= 3) & (wide < 6), -1.0, 0.0).astype(BF16)
     dq[...] = jnp.zeros_like(dq)
     dkv[...] = jnp.zeros_like(dkv)
+
+    build_ext(0, 0, 0)
+    build_ext(1, 0, 4)
     tile(0, 0, 1, diagonal=True)
+    kv_here(0, 1)
+    kv_near(1)
+    q_go(1, 4, 2, DOWN)
+    q_go(0, 5, 3, UP)
+    kv_here(7, 0)
+    kv_here(1, 0)
     tile(0, 1, 3)
 
     def before_0():
-        for rel, column in ORDER[4:8]:
-            kv_pass(rel, column)
+        kv_far(6, 0)
+        kv_far(2, 0)
+        kv_here(7, 1)
+        kv_here(1, 1)
 
     def before_1():
+        q_here(2)
+        q_go(2, 6, 4, DOWN)
+        q_here(3)
+        q_go(3, 7, 5, UP)
         for n in (1, 2):
             arrived(aux.at[n], aux_recv.at[n])
-        q_go(0, 6, 4, ACROSS)
-        q_go(1, 7, 5, ACROSS)
-        q_here(2)
-        q_here(3)
         build_ext(2, 1, 0)
         build_ext(3, 2, 4)
 
     def before_2():
-        kv_pass(6, 1)
-        kv_pass(2, 1)
-        kv_pass(5, 0)
+        kv_far(6, 1)
+        kv_far(2, 1)
+
+    def before_3():
+        kv_here(5, 0)
         kv_here(3, 0)
-
-    def before_4():
-        kv_pass(3, 1)
 
     def before_5():
         q_here(4)
@@ -358,12 +367,11 @@
         build_ext(4, 1, 4)
         build_ext(5, 2, 0)
 
-    def before_6():
-        kv_here(5, 1)
-        kv_here(4, 0)
-        kv_here(4, 1)
-
-    def before_8():
+    def before_7():
+        for rel, column in ORDER[12:]:
+            kv_here(rel, column)
+
+    def before_9():
         dq_go(2, UP)
         dq_go(3, DOWN)
 
@@ -387,17 +395,17 @@
         dq_go(5, DOWN)
 
     def before_14():
-        for rel, column in ((7, 1), (1, 1), (6, 0), (2, 0)):
+        for rel, column in ((6, 0), (2, 0), (7, 1), (1, 1)):
             reduce_go(rel, column)
 
     between = {
         0: before_0,
         1: before_1,
         2: before_2,
-        4: before_4,
+        3: before_3,
         5: before_5,
-        6: before_6,
-        8: before_8,
+        7: before_7,
+        9: before_9,
         10: before_10,
         11: before_11,
         12: before_12,
@@ -414,10 +422,10 @@
 
     lax.fori_loop(0, len(PAIRS), step, (jnp.int32(packed(PAIRS)), jnp.int32(packed(GROUPS))))
 
+    reduce_go(7, 0)
+    reduce_go(1, 0)
     dq_go(6, ACROSS)
     dq_go(7, ACROSS)
-    reduce_go(7, 0)
-    reduce_go(1, 0)
     r = rows(1, ROWS)
     dkv[r, :] = own_total(1)
     send(lambda: dkv.at[rows(1, ROWS)], lambda: xr, lambda: x_send, lambda: x_recv, OTHER)
@@ -435,6 +443,17 @@
         dq_out[rows(u, UNIT), :] = (total * scale).astype(BF16)
     for copy in pending:
         copy().wait_send()
+
+
+def hand_over(dq_in, dk_in, dv_in, dq_out, dk_out, dv_out, sems):
+    copies = [
+        pltpu.make_async_copy(src, dst, sems.at[n])
+        for n, (src, dst) in enumerate(((dq_in, dq_out), (dk_in, dk_out), (dv_in, dv_out)))
+    ]
+    for copy in copies:
+        copy.start()
+    for copy in copies:
+        copy.wait()
 
 
 def body(
@@ -456,13 +475,14 @@
     dma = pltpu.SemaphoreType.DMA
     units = 8 * UNIT
     keys = 16 * ROWS
-    query_grad, key_grad, value_grad = pl.pallas_call(
+    grads = (
+        jax.ShapeDtypeStruct(flat, BF16),
+        jax.ShapeDtypeStruct((tokens, width), BF16),
+        jax.ShapeDtypeStruct((tokens, width), BF16),
+    )
+    held = pl.pallas_call(
         kernel,
-        out_shape=(
-            jax.ShapeDtypeStruct(flat, BF16),
-            jax.ShapeDtypeStruct((tokens, width), BF16),
-            jax.ShapeDtypeStruct((tokens, width), BF16),
-        ),
+        out_shape=grads,
         in_specs=[hbm, hbm, vmem, vmem, vmem, vmem, smem, smem, smem],
         out_specs=(vmem, vmem, vmem),
         scratch_shapes=[
@@ -482,7 +502,7 @@
             pltpu.VMEM((6 * UNIT, width), BF16),
             pltpu.VMEM((6 * UNIT, width), BF16),
             dma((2, 2)),
-            dma((3, 16)),
+            dma((5, 16)),
             dma((16,)),
             dma((6, 2)),
             dma((8, 2)),
@@ -516,6 +536,14 @@
         value_exponent,
         span_order,
     )
+    query_grad, key_grad, value_grad = pl.pallas_call(
+        hand_over,
+        out_shape=grads,
+        in_specs=[hbm] * 3,
+        out_specs=(vmem, vmem, vmem),
+        scratch_shapes=[dma((3,))],
+        name="hand_over",
+    )(*held)
     return query_grad.reshape(heads, tokens, width), key_grad, value_grad
 
 

time: 66.7 us -> 63.1 us (0.946)
  local copies, waits for them, and re-layouts: 3.06 us -> 0 us
    unnamed x7 -> x0, local copies, waits for them, and re-layouts: 3.06 us -> none
    pallas_call x1 -> x2, Pallas kernels: 62.3 us -> 62.3 us  [the longest x1 60.6 us: body(): pl.pallas_call(kernel, out_shape=grads, in_specs=[hbm, hbm, vmem, vmem, v...]
where the time goes in v2:
time: 63.1 us; the launch traced here: 63 us
  Pallas kernels  62.3 us (99%)
  between operations  0.64 us (1%)
    pallas_call x1, Pallas kernels, body(): pl.pallas_call(kernel, out_shape=grads, in_specs=[hbm, hbm, vmem, vmem, v...  60.6 us
    pallas_call x1, Pallas kernels, body(): pl.pallas_call(hand_over, out_shape=grads, in_specs=[hbm] * 3, out_specs=...  1.7 us

profile of v2, /device:TPU:2, one launch (start us, length us, event | category | flops | bytes accessed | tf_op | source)
XLA Modules:
  0.0 63.0 jit_solution(7836670992180082894)
XLA Ops:
  0.6 60.6 %attention_backward.1 = (bf16[1024,128]{1,0:T(8,128)(2,1)}, bf16[128,128]{1,0:T(8,128)(2,1)}, bf16[128,128]{1,0:T(8,128)(2,1)}) custom-call(bf16[1024,128]{1,0:T(8,128)(2,1)} %bitcast.4, bf16[1024,128]{1,0:T(8,128)(2,1)} %bitcast.5, bf16[1024,128]{1,0:T(8,128)(2,1)} %bitcast.6, f32[8,128]{1,0:T(8,128)} %lse_in.1, bf16[128,128]{1,0:T(8,128)(2,1)} %k_in.1, ...), custom_call_target="tpu_custom_call" | custom-call | flops 10737418240 | bytes 1048576 | tf_op jit(solution)/shard_map/attention_backward/pallas_call | solution.py:483
  61.3 1.7 %hand_over.1 = (bf16[1024,128]{1,0:T(8,128)(2,1)}, bf16[128,128]{1,0:T(8,128)(2,1)}, bf16[128,128]{1,0:T(8,128)(2,1)}) custom-call(bf16[1024,128]{1,0:T(8,128)(2,1)} %get-tuple-element.9.dq_in, bf16[128,128]{1,0:T(8,128)(2,1)} %get-tuple-element.10.dk_in, bf16[128,128]{1,0:T(8,128)(2,1)} %get-tuple-element.11.dv_in), custom_call_target="tpu_custom_call" | custom-call | tf_op jit(solution)/shard_map/hand_over/pallas_call | solution.py:539

commit v3 on v2

--- a/solution.py
+++ b/solution.py
@@ -430,10 +430,6 @@
     dkv[r, :] = own_total(1)
     send(lambda: dkv.at[rows(1, ROWS)], lambda: xr, lambda: x_send, lambda: x_recv, OTHER)
     mine = own_total(0)
-    arrived(xr, x_recv)
-    mine = mine + xr[...]
-    dk_out[...] = (mine[:, :WIDTH] * scale).astype(BF16)
-    dv_out[...] = mine[:, WIDTH:].astype(BF16)
     for u, terms in ((0, (2, 5, 6)), (1, (3, 4, 7))):
         total = dq[rows(u, UNIT), :]
         for n in terms:
@@ -441,6 +437,10 @@
             arrived(dqr.at[r], dq_recv.at[n - 2])
             total = total + dqr[r, :].astype(F32)
         dq_out[rows(u, UNIT), :] = (total * scale).astype(BF16)
+    arrived(xr, x_recv)
+    mine = mine + xr[...]
+    dk_out[...] = (mine[:, :WIDTH] * scale).astype(BF16)
+    dv_out[...] = mine[:, WIDTH:].astype(BF16)
     for copy in pending:
         copy().wait_send()
 

time: 63.1 us -> 62.9 us (level)
  no operation moved by 1% of the time
where the time goes in v3:
time: 62.9 us; the launch traced here: 62.8 us
  Pallas kernels  62.1 us (99%)
  between operations  0.64 us (1%)
    pallas_call x1, Pallas kernels, body(): pl.pallas_call(kernel, out_shape=grads, in_specs=[hbm, hbm, vmem, vmem, v...  60.4 us
    pallas_call x1, Pallas kernels, body(): pl.pallas_call(hand_over, out_shape=grads, in_specs=[hbm] * 3, out_specs=...  1.7 us

profile of v3, /device:TPU:2, one launch (start us, length us, event | category | flops | bytes accessed | tf_op | source)
XLA Modules:
  0.0 62.8 jit_solution(6480346324599907312)
XLA Ops:
  0.6 60.4 %attention_backward.1 = (bf16[1024,128]{1,0:T(8,128)(2,1)}, bf16[128,128]{1,0:T(8,128)(2,1)}, bf16[128,128]{1,0:T(8,128)(2,1)}) custom-call(bf16[1024,128]{1,0:T(8,128)(2,1)} %bitcast.4, bf16[1024,128]{1,0:T(8,128)(2,1)} %bitcast.5, bf16[1024,128]{1,0:T(8,128)(2,1)} %bitcast.6, f32[8,128]{1,0:T(8,128)} %lse_in.1, bf16[128,128]{1,0:T(8,128)(2,1)} %k_in.1, ...), custom_call_target="tpu_custom_call" | custom-call | flops 10737418240 | bytes 1048576 | tf_op jit(solution)/shard_map/attention_backward/pallas_call | solution.py:483
  61.1 1.7 %hand_over.1 = (bf16[1024,128]{1,0:T(8,128)(2,1)}, bf16[128,128]{1,0:T(8,128)(2,1)}, bf16[128,128]{1,0:T(8,128)(2,1)}) custom-call(bf16[1024,128]{1,0:T(8,128)(2,1)} %get-tuple-element.9.dq_in, bf16[128,128]{1,0:T(8,128)(2,1)} %get-tuple-element.10.dk_in, bf16[128,128]{1,0:T(8,128)(2,1)} %get-tuple-element.11.dv_in), custom_call_target="tpu_custom_call" | custom-call | tf_op jit(solution)/shard_map/hand_over/pallas_call | solution.py:539

commit v4 on v3

--- a/solution.py
+++ b/solution.py
@@ -107,6 +107,7 @@
     UP, DOWN, ACROSS = device(0, 1, 0), device(0, -1, 0), device(0, 2, 0)
     RIGHT, LEFT, OTHER = device(0, 0, 1), device(0, 0, -1), device(1, 0, 0)
     RIGHT2, LEFT2 = device(0, 0, 2), device(0, 0, -2)
+    OTHER_RIGHT, OTHER_LEFT = device(1, 0, 1), device(1, 0, -1)
 
     def rows(index, size):
         return pl.ds(index * size, size)
@@ -120,7 +121,7 @@
             loads[-1].start()
 
     barrier = pltpu.get_barrier_semaphore()
-    for peer in (UP, DOWN, ACROSS, RIGHT, LEFT, RIGHT2, LEFT2, OTHER):
+    for peer in (UP, DOWN, ACROSS, RIGHT, LEFT, RIGHT2, LEFT2, OTHER, OTHER_RIGHT, OTHER_LEFT):
         pl.semaphore_signal(barrier, inc=1, device_id=peer, device_id_type=MESH)
 
     def power(e):
@@ -132,7 +133,7 @@
         kv[r, :WIDTH] = (k_in[r, :].astype(F32) * power(kexp[b])).astype(BF16)
         kv[r, WIDTH:] = (v_in[r, :].astype(F32) * power(vexp[b])).astype(BF16)
 
-    pl.semaphore_wait(barrier, 8)
+    pl.semaphore_wait(barrier, 10)
 
     pending = []
 
@@ -151,7 +152,7 @@
         ).wait_recv()
 
     def kv_go(way, src, dst):
-        peer = (RIGHT, LEFT, OTHER, RIGHT2, LEFT2)[way]
+        peer = (RIGHT, LEFT, OTHER, RIGHT2, LEFT2, OTHER_RIGHT, OTHER_LEFT)[way]
         send(
             lambda: kv.at[rows(src, ROWS)],
             lambda: kv.at[rows(dst, ROWS)],
@@ -166,8 +167,13 @@
 
     def kv_near(column):
         s = slot(0, column)
-        for way, rel in ((0, 7), (1, 1), (3, 6), (4, 2)):
-            kv_go(way, s, slot(rel, column))
+        if column == 0:
+            kv_go(0, s, slot(7, 0))
+            kv_go(1, s, slot(1, 0))
+            kv_go(5, s, slot(7, 1))
+            kv_go(6, s, slot(1, 1))
+        kv_go(3, s, slot(6, column))
+        kv_go(4, s, slot(2, column))
 
     def kv_far(rel, column):
         kv_here(rel, column)
@@ -502,7 +508,7 @@
             pltpu.VMEM((6 * UNIT, width), BF16),
             pltpu.VMEM((6 * UNIT, width), BF16),
             dma((2, 2)),
-            dma((5, 16)),
+            dma((7, 16)),
             dma((16,)),
             dma((6, 2)),
             dma((8, 2)),

time: 62.9 us -> 66.2 us (1.052)
  Pallas kernels: 62.1 us -> 65.4 us
    pallas_call x1, Pallas kernels: 60.4 us -> 63.7 us  [body(): pl.pallas_call(kernel, out_shape=grads, in_specs=[hbm, hbm, vmem, vmem, v...]
where the time goes in v4:
time: 66.2 us; the launch traced here: 66.1 us
  Pallas kernels  65.4 us (99%)
    pallas_call x1, Pallas kernels, body(): pl.pallas_call(kernel, out_shape=grads, in_specs=[hbm, hbm, vmem, vmem, v...  63.7 us
    pallas_call x1, Pallas kernels, body(): pl.pallas_call(hand_over, out_shape=grads, in_specs=[hbm] * 3, out_specs=...  1.7 us

profile of v4, /device:TPU:2, one launch (start us, length us, event | category | flops | bytes accessed | tf_op | source)
XLA Modules:
  0.0 66.1 jit_solution(7324258285465566323)
XLA Ops:
  0.6 63.7 %attention_backward.1 = (bf16[1024,128]{1,0:T(8,128)(2,1)}, bf16[128,128]{1,0:T(8,128)(2,1)}, bf16[128,128]{1,0:T(8,128)(2,1)}) custom-call(bf16[1024,128]{1,0:T(8,128)(2,1)} %bitcast.4, bf16[1024,128]{1,0:T(8,128)(2,1)} %bitcast.5, bf16[1024,128]{1,0:T(8,128)(2,1)} %bitcast.6, f32[8,128]{1,0:T(8,128)} %lse_in.1, bf16[128,128]{1,0:T(8,128)(2,1)} %k_in.1, ...), custom_call_target="tpu_custom_call" | custom-call | flops 10737418240 | bytes 1048576 | tf_op jit(solution)/shard_map/attention_backward/pallas_call | solution.py:489
  64.4 1.7 %hand_over.1 = (bf16[1024,128]{1,0:T(8,128)(2,1)}, bf16[128,128]{1,0:T(8,128)(2,1)}, bf16[128,128]{1,0:T(8,128)(2,1)}) custom-call(bf16[1024,128]{1,0:T(8,128)(2,1)} %get-tuple-element.9.dq_in, bf16[128,128]{1,0:T(8,128)(2,1)} %get-tuple-element.10.dk_in, bf16[128,128]{1,0:T(8,128)(2,1)} %get-tuple-element.11.dv_in), custom_call_target="tpu_custom_call" | custom-call | tf_op jit(solution)/shard_map/hand_over/pallas_call | solution.py:545
